TPU v7x, 32 devices: a whole 2x2x4 slice. The times are simulated.
32 devices in a mesh: dp: 8 (over z, y), section: 4 (over x, core).
Axes of the slice: x: 2, y: 2, z: 4, core: 2. Of those that a mesh axis runs over, the one named last changes fastest.
Arguments:
- tokens: bfloat16 [8192, 1024], P('dp'), may hold values from -6 to 6
- doc_lengths: int32 [16, 4], P('dp'), may hold values from 1 to 256, 512 in all within a row
- first_weights: bfloat16 [4, 1024, 4096], P('section'), may hold values from -0.1875 to 0.1875
- down_weights: bfloat16 [4, 2048, 1024], P('section'), may hold values from -0.09375 to 0.09375
- norm_gains: float32 [4, 2, 1024], P('section'), may hold values from 0.5 to 1.5
- norm_biases: float32 [4, 2, 1024], P('section'), may hold values from -1.2 to 1.2
- cotangent: bfloat16 [8192, 1024], P('dp'), may hold values from -6 to 6
Outputs:
- section_outputs: bfloat16 [4, 8192, 1024], P('section', 'dp')
- input_grads: bfloat16 [4, 8192, 1024], P('section', 'dp')
- first_grad: float32 [4, 1024, 4096], P('section', 'dp')
- down_grad: float32 [4, 2048, 1024], P('section', 'dp')
- gain_grad: float32 [4, 2, 1024], P('section', None, 'dp')
- bias_grad: float32 [4, 2, 1024], P('section', None, 'dp')
Inputs may be any that keep to these rules, and one draw needn't show every extreme that they name: `doc_lengths`: each row's lengths add up to 512.
All inputs are finite; a program needn't handle non-finite values.
Results may differ from a plain program's by a relative error of at most 0.02.
Values may be sent and summed in bfloat16 or wider, within the bound.
A program may use at most 384 MiB of HBM per device.

v0:
```python
import jax
import jax.numpy as jnp
from jax import lax
from jax.sharding import PartitionSpec as P

HEADS = 16
HEAD = 64


eps = 1e-05
masked_value = -1e30


def from_behind(value, axis, by):
    length = lax.axis_size(axis)
    pairs = [(i, i + by) for i in range(length) if 0 <= i + by < length]
    return lax.ppermute(value, axis, pairs)


def normalize(inputs, gain, shift_bias):
    average = jnp.mean(inputs, axis=-1, keepdims=True)
    centered = inputs - average
    variance = jnp.mean(centered * centered, axis=-1, keepdims=True)
    return centered * lax.rsqrt(variance + eps) * gain + shift_bias


def allowed_pairs(lengths, row_len):
    ends = jnp.cumsum(lengths)
    places = jnp.arange(row_len, dtype=jnp.int32)
    segment = jnp.sum((places[:, None] >= ends[None, :]).astype(jnp.int32), axis=1)
    return (segment[:, None] == segment[None, :]) & (places[None, :] <= places[:, None])


def split_heads(matrix):
    return matrix.reshape(matrix.shape[0], HEADS, HEAD)


def contract_rows(left, right):
    return lax.dot_general(
        left, right, (((0,), (0,)), ((), ())), preferred_element_type=jnp.float32
    )


def contract_cols(left, right):
    return lax.dot_general(
        left, right, (((1,), (1,)), ((), ())), preferred_element_type=jnp.float32
    )


def local(tokens, doc_lengths, first_weights, down_weights, norm_gains, norm_biases, cotangent):
    section_count = lax.axis_size("section")
    section_index = lax.axis_index("section")
    parity = section_index % 2
    micro_count = doc_lengths.shape[0]
    row_len = tokens.shape[0] // micro_count
    model_width = tokens.shape[1]
    weight = first_weights[0]
    hidden_units = weight.shape[1]
    half_units = hidden_units // 2
    own_down = down_weights[0]
    partner_down = from_behind(own_down, "section", 1)
    gain_in, gain_out = (norm_gains[0, 0], norm_gains[0, 1])
    bias_in, bias_out = (norm_biases[0, 0], norm_biases[0, 1])
    score_scale = HEAD ** (-0.5)
    tick_count = micro_count + section_count - 1

    def norm_in(inputs, gain, shift_bias):
        return normalize(inputs, gain, shift_bias)

    def attention_forward(normed, lengths):
        projected = jnp.dot(
            normed, weight[:, : 3 * model_width], preferred_element_type=jnp.float32
        ).astype(jnp.bfloat16)
        query_heads = split_heads(projected[:, :model_width])
        key_heads = split_heads(projected[:, model_width : 2 * model_width])
        value_heads = split_heads(projected[:, 2 * model_width :])
        scores = (
            jnp.einsum("qhd,khd->hqk", query_heads, key_heads, preferred_element_type=jnp.float32)
            * score_scale
        )
        scores = jnp.where(allowed_pairs(lengths, row_len)[None], scores, masked_value)
        row_top = jnp.max(scores, axis=-1, keepdims=True)
        exponent = jnp.exp(scores - row_top)
        row_total = jnp.sum(exponent, axis=-1, keepdims=True)
        prob_low = (exponent / row_total).astype(jnp.bfloat16)
        context = jnp.einsum(
            "hqk,khd->qhd", prob_low, value_heads, preferred_element_type=jnp.float32
        )
        context = context.reshape(row_len, model_width).astype(jnp.bfloat16)
        branch = contract_cols(context, weight[:, 3 * model_width :])
        kept_big = jnp.concatenate([projected, context], axis=1).astype(jnp.float32)
        log_total = (row_top + jnp.log(row_total))[:, :, 0]
        return (branch, kept_big, log_total)

    def feed_forward(normed, lengths):
        hidden_pre = jnp.dot(normed, weight, preferred_element_type=jnp.float32)
        hidden = jax.nn.gelu(hidden_pre).astype(jnp.bfloat16)
        branch = jnp.dot(hidden[:, :half_units], partner_down, preferred_element_type=jnp.float32)
        branch = branch + jnp.dot(
            hidden[:, half_units:], own_down, preferred_element_type=jnp.float32
        )
        return (branch, hidden_pre, jnp.zeros((HEADS, row_len), jnp.float32))

    rows_in = tokens.reshape(micro_count, row_len, model_width)
    rows_cot = cotangent.reshape(micro_count, row_len, model_width)

    def forward_tick(step_index, carry):
        incoming = carry[0]
        position = step_index - section_index
        row_valid = (position >= 0) & (position < micro_count)
        slot_index = jnp.clip(position, 0, micro_count - 1)
        source = jnp.where(section_index == 0, rows_in[slot_index], incoming)
        lengths = doc_lengths[slot_index]

        def forward_run_rows(kept):
            kept_inputs, kept_branch, kept_big, kept_log, produced = kept
            current = source.astype(jnp.float32)
            normed = norm_in(current, gain_in, bias_in).astype(jnp.bfloat16)
            branch, big_rows, log_total = lax.cond(
                parity == 1, feed_forward, attention_forward, normed, lengths
            )
            output = (current + normalize(branch, gain_out, bias_out)).astype(jnp.bfloat16)
            updated = (
                kept_inputs.at[slot_index].set(source),
                kept_branch.at[slot_index].set(branch),
                kept_big.at[slot_index].set(big_rows),
                kept_log.at[slot_index].set(log_total),
                produced.at[slot_index].set(output),
            )
            return (updated, output)

        def forward_skip_rows(kept):
            return (kept, jnp.zeros((row_len, model_width), jnp.bfloat16))

        kept, output = lax.cond(row_valid, forward_run_rows, forward_skip_rows, carry[1:])
        arriving = from_behind(output, "section", 1)
        return (arriving,) + kept

    start = (
        jnp.zeros((row_len, model_width), jnp.bfloat16),
        jnp.zeros((micro_count, row_len, model_width), jnp.bfloat16),
        jnp.zeros((micro_count, row_len, model_width), jnp.float32),
        jnp.zeros((micro_count, row_len, hidden_units), jnp.float32),
        jnp.zeros((micro_count, HEADS, row_len), jnp.float32),
        jnp.zeros((micro_count, row_len, model_width), jnp.bfloat16),
    )
    forward_done = lax.fori_loop(0, tick_count, forward_tick, start)
    kept_inputs, kept_branch, kept_big, kept_log, produced = forward_done[1:]

    def feed_backward(operands):
        d_branch, normed, big_rows, log_total, lengths, acc_first, acc_down = operands
        hidden_full, gelu_back = jax.vjp(jax.nn.gelu, big_rows)
        hidden = hidden_full.astype(jnp.bfloat16)
        grad_upper = contract_rows(hidden[:, :half_units], d_branch)
        grad_lower = contract_rows(hidden[:, half_units:], d_branch)
        acc_down = acc_down + jnp.stack([grad_upper, grad_lower], axis=0)
        d_hidden = jnp.concatenate(
            [contract_cols(d_branch, partner_down), contract_cols(d_branch, own_down)], axis=1
        )
        d_pre = gelu_back(d_hidden)[0].astype(jnp.bfloat16)
        acc_first = acc_first + contract_rows(normed, d_pre)
        d_normed = contract_cols(d_pre, weight)
        return (d_normed, acc_first, acc_down)

    def attention_backward(operands):
        d_branch, normed, big_rows, log_total, lengths, acc_first, acc_down = operands
        projected = big_rows[:, : 3 * model_width].astype(jnp.bfloat16)
        context = big_rows[:, 3 * model_width :].astype(jnp.bfloat16)
        query_heads = split_heads(projected[:, :model_width])
        key_heads = split_heads(projected[:, model_width : 2 * model_width])
        value_heads = split_heads(projected[:, 2 * model_width :])
        d_out_proj = contract_rows(d_branch, context)
        d_context = jnp.dot(
            d_branch, weight[:, 3 * model_width :], preferred_element_type=jnp.float32
        ).astype(jnp.bfloat16)
        d_ctx_heads = split_heads(d_context)
        scores = (
            jnp.einsum("qhd,khd->hqk", query_heads, key_heads, preferred_element_type=jnp.float32)
            * score_scale
        )
        scores = jnp.where(allowed_pairs(lengths, row_len)[None], scores, masked_value)
        prob_full = jnp.exp(scores - log_total[:, :, None])
        prob_low = prob_full.astype(jnp.bfloat16)
        d_prob = jnp.einsum(
            "qhd,khd->hqk", d_ctx_heads, value_heads, preferred_element_type=jnp.float32
        )
        d_values = jnp.einsum(
            "hqk,qhd->khd", prob_low, d_ctx_heads, preferred_element_type=jnp.float32
        )
        d_scores = (
            prob_full * (d_prob - jnp.sum(d_prob * prob_full, axis=-1, keepdims=True))
        ).astype(jnp.bfloat16)
        d_query = (
            jnp.einsum("hqk,khd->qhd", d_scores, key_heads, preferred_element_type=jnp.float32)
            * score_scale
        )
        d_keys = (
            jnp.einsum("hqk,qhd->khd", d_scores, query_heads, preferred_element_type=jnp.float32)
            * score_scale
        )
        d_projected = jnp.concatenate(
            [
                d_query.reshape(row_len, model_width),
                d_keys.reshape(row_len, model_width),
                d_values.reshape(row_len, model_width),
            ],
            axis=1,
        ).astype(jnp.bfloat16)
        acc_first = acc_first + jnp.concatenate(
            [contract_rows(normed, d_projected), d_out_proj], axis=1
        )
        d_normed = contract_cols(d_projected, weight[:, : 3 * model_width])
        return (d_normed, acc_first, acc_down)

    def backward_tick(step_index, carry):
        incoming = carry[0]
        position = step_index - (section_count - 1 - section_index)
        row_valid = (position >= 0) & (position < micro_count)
        slot_index = jnp.clip(position, 0, micro_count - 1)
        upstream = jnp.where(section_index == section_count - 1, rows_cot[slot_index], incoming)

        def backward_run_rows(accs):
            acc_first, acc_down, acc_gain, acc_bias, returned = accs
            current = kept_inputs[slot_index].astype(jnp.float32)
            grad_out = upstream.astype(jnp.float32)
            out_back = jax.vjp(normalize, kept_branch[slot_index], gain_out, bias_out)[1]
            d_branch, d_gain_out, d_bias_out = out_back(grad_out)
            normed_full, in_back = jax.vjp(normalize, current, gain_in, bias_in)
            normed = normed_full.astype(jnp.bfloat16)
            operands = (
                d_branch.astype(jnp.bfloat16),
                normed,
                kept_big[slot_index],
                kept_log[slot_index],
                doc_lengths[slot_index],
                acc_first,
                acc_down,
            )
            d_normed, acc_first, acc_down = lax.cond(
                parity == 1, feed_backward, attention_backward, operands
            )
            d_current, d_gain_in, d_bias_in = in_back(d_normed)
            d_input = (grad_out + d_current).astype(jnp.bfloat16)
            acc_gain = acc_gain + jnp.stack([d_gain_in, d_gain_out], axis=0)
            acc_bias = acc_bias + jnp.stack([d_bias_in, d_bias_out], axis=0)
            return (
                (acc_first, acc_down, acc_gain, acc_bias, returned.at[slot_index].set(d_input)),
                d_input,
            )

        def backward_skip_rows(accs):
            return (accs, jnp.zeros((row_len, model_width), jnp.bfloat16))

        accs, d_input = lax.cond(row_valid, backward_run_rows, backward_skip_rows, carry[1:])
        arriving = from_behind(d_input, "section", -1)
        return (arriving,) + accs

    start_back = (
        jnp.zeros((row_len, model_width), jnp.bfloat16),
        jnp.zeros((model_width, hidden_units), jnp.float32),
        jnp.zeros((2, half_units, model_width), jnp.float32),
        jnp.zeros((2, model_width), jnp.float32),
        jnp.zeros((2, model_width), jnp.float32),
        jnp.zeros((micro_count, row_len, model_width), jnp.bfloat16),
    )
    backward_done = lax.fori_loop(0, tick_count, backward_tick, start_back)
    acc_first, acc_down, acc_gain, acc_bias, returned = backward_done[1:]
    arriving = from_behind(acc_down[0].astype(jnp.bfloat16), "section", -1).astype(jnp.float32)
    own_grad = jnp.where(parity == 1, acc_down[1], arriving)
    first_part, down_part, gain_part, bias_part = (
        lax.psum_scatter(acc_first, "dp", scatter_dimension=0, tiled=True),
        lax.psum_scatter(own_grad, "dp", scatter_dimension=0, tiled=True),
        lax.psum_scatter(acc_gain, "dp", scatter_dimension=1, tiled=True),
        lax.psum_scatter(acc_bias, "dp", scatter_dimension=1, tiled=True),
    )
    section_outputs = produced.reshape(1, micro_count * row_len, model_width)
    input_grads = returned.reshape(1, micro_count * row_len, model_width)
    return (
        section_outputs,
        input_grads,
        first_part[None],
        down_part[None],
        gain_part[None],
        bias_part[None],
    )


def solution(mesh):
    placed = (
        P("dp", None),
        P("dp", None),
        P("section", None, None),
        P("section", None, None),
        P("section", None, None),
        P("section", None, None),
        P("dp", None),
    )
    return jax.shard_map(
        local,
        mesh=mesh,
        in_specs=placed,
        out_specs=(
            P("section", "dp", None),
            P("section", "dp", None),
            P("section", "dp", None),
            P("section", "dp", None),
            P("section", None, "dp"),
            P("section", None, "dp"),
        ),
        check_vma=False,
    )
```

profile of v0, /device:TPU:0, one launch (start us, length us, event | category | flops | bytes accessed | tf_op | source)
XLA Modules:
  0.0 1679.5 jit_solution(6719161925538909955)
XLA Ops:
  20.9 7.8 broadcast_in_dim.108
  30.9 377.9 %while.55 = (s32[]{:T(128)}, bf16[512,1024]{1,0:T(8,128)(2,1)S(1)}, bf16[2,512,1024]{2,1,0:T(8,128)(2,1)}, f32[2,512,1024]{2,1,0:T(8,128)}, f32[2,512,4096]{2,1,...) while((s32[]{:T(128)}, bf16[512,1024]{1,0:T(8,128)(2,1)S(1)}, ...), condition=%wide.region_14.15_spmd, body=%wide.region_0.14_spmd.sunk | while | flops 8625595392 | bytes 212234144 | solution.py:147
  30.9 89.0 %conditional.6 = (bf16[2,512,1024]{2,1,0:T(8,128)(2,1)}, f32[2,512,1024]{2,1,0:T(8,128)}, f32[2,512,4096]{2,1,0:T(8,128)}, f32[2,16,512]{2,1,0:T(8,128)}, bf16[2...) conditional(s32[]{:T(128)} %convert_element_type.252, (bf16[2,512,1024]{2,1,0:T(8,128)(2,1)}, ...), branch_computations={%region_1.1_spmd, %region_2.13_spmd} | conditional | flops 8625595392 | bytes 208039376 | solution.py:135
  35.5 57.8 %conditional = (f32[512,1024]{1,0:T(8,128)}, f32[1,512,4096]{2,1,0:T(8,128)}, f32[1,16,512]{2,1,0:T(8,128)S(1)}, f32[]{:T(128)}, f32[1,512,1024]{2,1,0:T(8,128)}) conditional(s32[]{:T(128)} %convert_element_type.136, (bf16[1024,4096]{1,0:T(8,128)(2,1)}, bf16[512,1024]{1,0:T(8,128)(2,1)S(1)}, s32[2,4]{1,0:T(2,128)}, s32[]{:T(128)}) %tuple.117, ...), branch_computations={%region_6.9_spmd, %region_11.10_spmd} | conditional | flops 8609333248 | bytes 123998424 | solution.py:119
  35.5 6.4 fusion.5
  51.6 8.6 fusion
  60.2 9.3 fusion.1
  69.4 8.4 fusion.10
  105.3 12.6 select_dynamic-update-slice_fusion
  123.7 89.0 %conditional.6 = (bf16[2,512,1024]{2,1,0:T(8,128)(2,1)}, f32[2,512,1024]{2,1,0:T(8,128)}, f32[2,512,4096]{2,1,0:T(8,128)}, f32[2,16,512]{2,1,0:T(8,128)}, bf16[2...) conditional(s32[]{:T(128)} %convert_element_type.252, (bf16[2,512,1024]{2,1,0:T(8,128)(2,1)}, ...), branch_computations={%region_1.1_spmd, %region_2.13_spmd} | conditional | flops 8625595392 | bytes 208039376 | solution.py:135
  128.3 57.8 %conditional = (f32[512,1024]{1,0:T(8,128)}, f32[1,512,4096]{2,1,0:T(8,128)}, f32[1,16,512]{2,1,0:T(8,128)S(1)}, f32[]{:T(128)}, f32[1,512,1024]{2,1,0:T(8,128)}) conditional(s32[]{:T(128)} %convert_element_type.136, (bf16[1024,4096]{1,0:T(8,128)(2,1)}, bf16[512,1024]{1,0:T(8,128)(2,1)S(1)}, s32[2,4]{1,0:T(2,128)}, s32[]{:T(128)}) %tuple.117, ...), branch_computations={%region_6.9_spmd, %region_11.10_spmd} | conditional | flops 8609333248 | bytes 123998424 | solution.py:119
  128.3 6.4 fusion.5
  144.3 8.6 fusion
  152.9 9.3 fusion.1
  162.2 8.4 fusion.10
  198.1 12.6 select_dynamic-update-slice_fusion
  217.5 55.7 %collective-permute-start = (bf16[512,1024]{1,0:T(8,128)(2,1)}, bf16[512,1024]{1,0:T(8,128)(2,1)S(1)}, u32[]{:S(2)}, u32[]{:S(2)}) collective-permute-start(bf16[512,1024]{1,0:T(8,128)(2,1)} %get-tuple-element.1901), channel_id=1, source_target_pairs={{0,1},{1,2},{2,3},{4,5},{5,6},{6,7},{8,9},{9,10},{10,11},{12,13},{... | collective-permute-start | bytes 3145736 | tf_op jit(solution)/shard_map/while/body/eval_jaxpr/ppermute | solution.py:17
  276.8 24.1 %collective-permute-start = (bf16[512,1024]{1,0:T(8,128)(2,1)}, bf16[512,1024]{1,0:T(8,128)(2,1)S(1)}, u32[]{:S(2)}, u32[]{:S(2)}) collective-permute-start(bf16[512,1024]{1,0:T(8,128)(2,1)} %get-tuple-element.1901), channel_id=1, source_target_pairs={{0,1},{1,2},{2,3},{4,5},{5,6},{6,7},{8,9},{9,10},{10,11},{12,13},{... | collective-permute-start | bytes 3145736 | tf_op jit(solution)/shard_map/while/body/eval_jaxpr/ppermute | solution.py:17
  304.4 101.8 %collective-permute-start = (bf16[512,1024]{1,0:T(8,128)(2,1)}, bf16[512,1024]{1,0:T(8,128)(2,1)S(1)}, u32[]{:S(2)}, u32[]{:S(2)}) collective-permute-start(bf16[512,1024]{1,0:T(8,128)(2,1)} %get-tuple-element.1901), channel_id=1, source_target_pairs={{0,1},{1,2},{2,3},{4,5},{5,6},{6,7},{8,9},{9,10},{10,11},{12,13},{... | collective-permute-start | bytes 3145736 | tf_op jit(solution)/shard_map/while/body/eval_jaxpr/ppermute | solution.py:17
  409.0 7.9 broadcast_in_dim.110
  416.9 7.9 broadcast_in_dim.111
  427.5 668.6 %while.56 = (s32[]{:T(128)}, bf16[512,1024]{1,0:T(8,128)(2,1)S(1)}, f32[1024,4096]{0,1:T(8,128)}, f32[2,2048,1024]{2,1,0:T(8,128)}, f32[2,1024]{1,0:T(2,128)}, /...) while((s32[]{:T(128)}, bf16[512,1024]{1,0:T(8,128)(2,1)S(1)}, ...), condition=%wide.region_36.37_spmd, body=%wide.region_15.36_spmd.sunk | while | flops 17271107584 | bytes 569214400 | solution.py:266
  427.9 7.0 conditional.7
  436.2 14.9 collective-permute-done.1
  453.7 45.6 %collective-permute-done.1 = bf16[512,1024]{1,0:T(8,128)(2,1)S(1)} collective-permute-done((bf16[512,1024]{1,0:T(8,128)(2,1)}, bf16[512,1024]{1,0:T(8,128)(2,1)S(1)}, u32[]{:S(2)}, u32[]{:S(2)}) %collective-permute-start.1) | collective-permute-done | bytes 1048608 | tf_op jit(solution)/shard_map/while/body/eval_jaxpr/ppermute | solution.py:17
  501.7 322.6 %collective-permute-done.1 = bf16[512,1024]{1,0:T(8,128)(2,1)S(1)} collective-permute-done((bf16[512,1024]{1,0:T(8,128)(2,1)}, bf16[512,1024]{1,0:T(8,128)(2,1)S(1)}, u32[]{:S(2)}, u32[]{:S(2)}) %collective-permute-start.1) | collective-permute-done | bytes 1048608 | tf_op jit(solution)/shard_map/while/body/eval_jaxpr/ppermute | solution.py:17
  824.2 128.6 %conditional.7 = (f32[1024,4096]{0,1:T(8,128)}, f32[2,2048,1024]{2,1,0:T(8,128)}, f32[2,1024]{1,0:T(2,128)}, f32[2,1024]{1,0:T(2,128)}, bf16[2,512,1024]{2,1,0:T(8,128)(2,1)}, /*index=5*/bf16[512,1024]{1,0:T(8,128)(2,1)}) conditional(s32[]{:T(128)} %convert_element_type.253, (f32[1024,4096]{0,1:T(8,128)}, f32[2,2048,1024]{2,1,0:T(8,128)}, ...), branch_computations={%region_16.16_spmd, %region_17.35_spmd} | conditional | flops 17271107584 | bytes 565019648 | solution.py:254
  824.2 7.7 dynamic-slice_bitcast_fusion.3
  842.0 98.1 %conditional.2 = (f32[512,1024]{1,0:T(8,128)S(1)}, f32[1024,4096]{0,1:T(8,128)}, f32[2,2048,1024]{2,1,0:T(8,128)}) conditional(s32[]{:T(128)} %convert_element_type.147, (s32[2,4]{1,0:T(2,128)}, s32[]{:T(128)}, f32[512,4096]{1,0:T(8,128)}, f32[2,16,512]{2,1,0:T(8,128)}, bf16[1024,4096]{1,0:T(8,128)(2,1)}, ...), branch_computations={%region_24.26_spmd, %region_28.27_spmd} | conditional | flops 17240686592 | bytes 469406304 | solution.py:239
  846.5 7.4 copy.56
  872.0 11.0 multiply_reduce_fusion.1
  883.0 11.9 multiply_convert_fusion
  908.3 10.0 convolution_bitcast_fusion
  918.3 8.7 maximum_add_fusion
  959.3 129.0 %conditional.7 = (f32[1024,4096]{0,1:T(8,128)}, f32[2,2048,1024]{2,1,0:T(8,128)}, f32[2,1024]{1,0:T(2,128)}, f32[2,1024]{1,0:T(2,128)}, bf16[2,512,1024]{2,1,0:T(8,128)(2,1)}, /*index=5*/bf16[512,1024]{1,0:T(8,128)(2,1)}) conditional(s32[]{:T(128)} %convert_element_type.253, (f32[1024,4096]{0,1:T(8,128)}, f32[2,2048,1024]{2,1,0:T(8,128)}, ...), branch_computations={%region_16.16_spmd, %region_17.35_spmd} | conditional | flops 17271107584 | bytes 565019648 | solution.py:254
  959.3 7.8 dynamic-slice_bitcast_fusion.3
  977.1 98.4 %conditional.2 = (f32[512,1024]{1,0:T(8,128)S(1)}, f32[1024,4096]{0,1:T(8,128)}, f32[2,2048,1024]{2,1,0:T(8,128)}) conditional(s32[]{:T(128)} %convert_element_type.147, (s32[2,4]{1,0:T(2,128)}, s32[]{:T(128)}, f32[512,4096]{1,0:T(8,128)}, f32[2,16,512]{2,1,0:T(8,128)}, bf16[1024,4096]{1,0:T(8,128)(2,1)}, ...), branch_computations={%region_24.26_spmd, %region_28.27_spmd} | conditional | flops 17240686592 | bytes 469406304 | solution.py:239
  981.9 7.4 copy.56
  1007.4 11.0 multiply_reduce_fusion.1
  1018.4 12.2 multiply_convert_fusion
  1044.0 10.0 convolution_bitcast_fusion
  1054.0 8.7 maximum_add_fusion
  1111.6 10.1 bitcast_select_fusion.5
  1121.9 17.6 %copy.57 = f32[1024,4096]{1,0:T(8,128)} copy(f32[1024,4096]{0,1:T(8,128)} %get-tuple-element.1501) | data formatting | bytes 33554432 | tf_op jit(solution)/shard_map/while | solution.py:266
  1139.4 30.1 %reduce-scatter.13.cloned.1.call-done = f32[128,2]{1,0:T(8,128)} async-done(((f32[1024,2]{1,0:T(8,128)}), f32[128,2]{1,0:T(8,128)}) %reduce-scatter.13.cloned.1.call-update) | async-done | bytes 1040
  1171.0 63.2 %reduce-scatter.15.cloned.1.call-done = f32[128,2]{1,0:T(8,128)} async-done(((f32[1024,2]{1,0:T(8,128)}), f32[128,2]{1,0:T(8,128)}) %reduce-scatter.15.cloned.1.call-update) | async-done | bytes 1040
  1235.7 150.8 %reduce-scatter.11.cloned.1.call-done = f32[256,1024]{1,0:T(8,128)} async-done(((f32[2048,1024]{1,0:T(8,128)}), f32[256,1024]{1,0:T(8,128)}) %reduce-scatter.11.cloned.1.call-update) | async-done | bytes 1048592 | tf_op jit(solution)/shard_map/reduce_scatter | solution.py:272
  1386.5 285.8 %reduce-scatter.9.cloned.1.call-done = f32[128,4096]{1,0:T(8,128)} async-done(((f32[1024,4096]{1,0:T(8,128)}), f32[128,4096]{1,0:T(8,128)}) %reduce-scatter.9.cloned.1.call-update) | async-done | bytes 2097168 | tf_op jit(solution)/shard_map/reduce_scatter | solution.py:271
  (288 shorter events, 294.2 us)
Async XLA Ops:
  7.2 1162.4 %reduce-scatter.13.cloned.1.call-start = ((), (), s32[]{:S(2)}) async-start(), calls=%async_computation.6 | async-start | bytes 589824
  7.2 9.5 collective-permute-start.2
  60.2 9.3 copy-start.16
  77.8 4.6 copy-start.17
  97.1 5.5 copy-start.3
  105.3 12.6 copy-start.4
  119.9 3.8 collective-permute-start
  152.9 9.3 copy-start.16
  170.6 4.6 copy-start.17
  189.8 5.5 copy-start.3
  198.1 12.6 copy-start.4
  212.7 3.8 collective-permute-start
  217.5 58.2 %collective-permute-start = (bf16[512,1024]{1,0:T(8,128)(2,1)}, bf16[512,1024]{1,0:T(8,128)(2,1)S(1)}, u32[]{:S(2)}, u32[]{:S(2)}) collective-permute-start(bf16[512,1024]{1,0:T(8,128)(2,1)} %get-tuple-element.1901), channel_id=1, source_target_pairs={{0,1},{1,2},{2,3},{4,5},{5,6},{6,7},{8,9},{9,10},{10,11},{12,13},{... | collective-permute-start | bytes 3145736 | tf_op jit(solution)/shard_map/while/body/eval_jaxpr/ppermute | solution.py:17
  276.8 26.5 %collective-permute-start = (bf16[512,1024]{1,0:T(8,128)(2,1)}, bf16[512,1024]{1,0:T(8,128)(2,1)S(1)}, u32[]{:S(2)}, u32[]{:S(2)}) collective-permute-start(bf16[512,1024]{1,0:T(8,128)(2,1)} %get-tuple-element.1901), channel_id=1, source_target_pairs={{0,1},{1,2},{2,3},{4,5},{5,6},{6,7},{8,9},{9,10},{10,11},{12,13},{... | collective-permute-start | bytes 3145736 | tf_op jit(solution)/shard_map/while/body/eval_jaxpr/ppermute | solution.py:17
  304.4 104.2 %collective-permute-start = (bf16[512,1024]{1,0:T(8,128)(2,1)}, bf16[512,1024]{1,0:T(8,128)(2,1)S(1)}, u32[]{:S(2)}, u32[]{:S(2)}) collective-permute-start(bf16[512,1024]{1,0:T(8,128)(2,1)} %get-tuple-element.1901), channel_id=1, source_target_pairs={{0,1},{1,2},{2,3},{4,5},{5,6},{6,7},{8,9},{9,10},{10,11},{12,13},{... | collective-permute-start | bytes 3145736 | tf_op jit(solution)/shard_map/while/body/eval_jaxpr/ppermute | solution.py:17
  434.9 16.2 collective-permute-start.1
  452.4 46.9 %collective-permute-start.1 = (bf16[512,1024]{1,0:T(8,128)(2,1)}, bf16[512,1024]{1,0:T(8,128)(2,1)S(1)}, u32[]{:S(2)}, u32[]{:S(2)}) collective-permute-start(bf16[512,1024]{1,0:T(8,128)(2,1)} %get-tuple-element.1929), channel_id=1, source_target_pairs={{1,0},{2,1},{3,2},{5,4},{6,5},{7,6},{9,8},{10,9},{11,10},{13,12},{... | collective-permute-start | bytes 3145736 | tf_op jit(solution)/shard_map/while/body/eval_jaxpr/ppermute | solution.py:17
  500.4 323.8 %collective-permute-start.1 = (bf16[512,1024]{1,0:T(8,128)(2,1)}, bf16[512,1024]{1,0:T(8,128)(2,1)S(1)}, u32[]{:S(2)}, u32[]{:S(2)}) collective-permute-start(bf16[512,1024]{1,0:T(8,128)(2,1)} %get-tuple-element.1929), channel_id=1, source_target_pairs={{1,0},{2,1},{3,2},{5,4},{6,5},{7,6},{9,8},{10,9},{11,10},{13,12},{... | collective-permute-start | bytes 3145736 | tf_op jit(solution)/shard_map/while/body/eval_jaxpr/ppermute | solution.py:17
  824.2 7.8 copy-start.5
  865.9 6.2 copy-start
  883.0 11.9 copy-start.23
  899.1 6.4 copy-start.19
  899.1 19.1 %slice-start = ((s8[16777216]{0:T(1024)(128)(4,1)}), s8[4194304]{0:T(1024)(128)(4,1)S(1)}, s32[]{:S(2)}) async-start(s8[16777216]{0:T(1024)(128)(4,1)} %bitcast.165), calls=%async_computation.8 | async-start | bytes 8388608 | tf_op jit(solution)/shard_map/while/body/eval_jaxpr/cond/branch_1_fun/cond
  899.1 19.1 %slice-start.1 = ((s8[16777216]{0:T(1024)(128)(4,1)}), s8[4194304]{0:T(1024)(128)(4,1)S(1)}, s32[]{:S(2)}) async-start(s8[16777216]{0:T(1024)(128)(4,1)} %bitcast.165), calls=%async_computation.9 | async-start | bytes 8388608 | tf_op jit(solution)/shard_map/while/body/eval_jaxpr/cond/branch_1_fun/cond
  905.6 12.7 slice-start.2
  908.3 10.0 slice-start.3
  927.0 5.7 copy-start.1
  940.1 8.9 copy-start.9
  940.1 8.9 copy-start.24
  952.9 6.1 collective-permute-start.1
  959.3 7.8 copy-start.5
  1001.3 6.2 copy-start
  1018.4 12.2 copy-start.23
  1034.8 6.4 copy-start.19
  1034.8 19.1 %slice-start = ((s8[16777216]{0:T(1024)(128)(4,1)}), s8[4194304]{0:T(1024)(128)(4,1)S(1)}, s32[]{:S(2)}) async-start(s8[16777216]{0:T(1024)(128)(4,1)} %bitcast.165), calls=%async_computation.8 | async-start | bytes 8388608 | tf_op jit(solution)/shard_map/while/body/eval_jaxpr/cond/branch_1_fun/cond
  1034.9 19.1 %slice-start.1 = ((s8[16777216]{0:T(1024)(128)(4,1)}), s8[4194304]{0:T(1024)(128)(4,1)S(1)}, s32[]{:S(2)}) async-start(s8[16777216]{0:T(1024)(128)(4,1)} %bitcast.165), calls=%async_computation.9 | async-start | bytes 8388608 | tf_op jit(solution)/shard_map/while/body/eval_jaxpr/cond/branch_1_fun/cond
  1041.3 12.7 slice-start.2
  1044.0 10.0 slice-start.3
  1062.7 5.7 copy-start.1
  1075.5 8.9 copy-start.9
  1075.5 8.9 copy-start.24
  1088.3 4.8 collective-permute-start.1
  1096.1 7.4 copy-start.28
  1096.1 8.5 copy-start.29
  1102.3 9.4 collective-permute-start.3
  1104.6 129.6 %reduce-scatter.15.cloned.1.call-start = ((), (), s32[]{:S(2)}) async-start(), calls=%async_computation.7 | async-start | bytes 589824
  1105.7 280.8 %reduce-scatter.11.cloned.1.call-start = ((), (), s32[]{:S(2)}) async-start(), calls=%async_computation.5 | async-start | bytes 9437184 | tf_op jit(solution)/shard_map/reduce_scatter | solution.py:272
  1121.8 550.6 %reduce-scatter.9.cloned.1.call-start = ((), (), s32[]{:S(2)}) async-start(), calls=%async_computation.4 | async-start | bytes 18874368 | tf_op jit(solution)/shard_map/reduce_scatter | solution.py:271
  (24 other events, 48.3 us)
Sparse Core Ops, SparseCore 0:
  1104.7 64.7 reduce-scatter.12
  1173.2 60.9 reduce-scatter.14
  1238.4 148.0 reduce-scatter.10
  1391.2 281.1 reduce-scatter.8
where the time goes:
time: 1700 us; the launch traced here: 1680 us
  waiting for transfers between devices  943 us (55%)
  starting transfers between devices  197 us (12%)
  other arithmetic  189 us (11%)
  local copies, waits for them, and re-layouts  160 us (9%)
  matrix products  150 us (9%)
  loops' own time  26.4 us (2%)
    ppermute x12, waiting for transfers between devices, from_behind(): return lax.ppermute(value, axis, pairs)  413 us
    reduce_scatter x1, waiting for transfers between devices, local(): lax.psum_scatter(acc_first, 'dp', scatter_dimension=0, tiled=True)  286 us
    ppermute x12, starting transfers between devices, from_behind(): return lax.ppermute(value, axis, pairs)  196 us
    reduce_scatter x1, waiting for transfers between devices, local(): lax.psum_scatter(own_grad, 'dp', scatter_dimension=0, tiled=True)  151 us
    unnamed x6, waiting for transfers between devices  93.4 us
  transfers between devices with their start and end apart: 16, of which 16 were waited for; matrix products, arithmetic and copies ran while one was open for 2% of the time, Pallas kernels for 0%

commit v1 on v0

v1 whole, which is shorter than its diff:
```python
import functools

import jax
import jax.numpy as jnp
from jax import lax
from jax.experimental import pallas as pl
from jax.experimental.pallas import tpu as pltpu
from jax.sharding import PartitionSpec as P

HEADS = 16
HEAD = 64
eps = 1e-05
masked_value = -1e30
MESH = pl.DeviceIdType.MESH


def swap_pair(value):
    length = lax.axis_size("section")
    return lax.ppermute(value, "section", [(i, i ^ 1) for i in range(length)])


def hop(value, by):
    length = lax.axis_size("section")
    pairs = [(i, i + by) for i in range(length) if 0 <= i + by < length]
    return lax.ppermute(value, "section", pairs)


def normalize(inputs, gain, shift_bias):
    average = jnp.mean(inputs, axis=-1, keepdims=True)
    centered = inputs - average
    variance = jnp.mean(centered * centered, axis=-1, keepdims=True)
    return centered * lax.rsqrt(variance + eps) * gain + shift_bias


def allowed_pairs(lengths, row_len):
    ends = jnp.cumsum(lengths)
    places = jnp.arange(row_len, dtype=jnp.int32)
    segment = jnp.sum((places[:, None] >= ends[None, :]).astype(jnp.int32), axis=1)
    return (segment[:, None] == segment[None, :]) & (places[None, :] <= places[:, None])


def split_heads(matrix):
    return matrix.reshape(matrix.shape[0], HEADS, HEAD)


def contract_cols(left, right):
    return lax.dot_general(
        left, right, (((1,), (1,)), ((), ())), preferred_element_type=jnp.float32
    )


def ring_place(index, count):
    return jnp.where(index % 2 == 0, index // 2, count - 1 - index // 2)


def ring_index(place, count):
    return jnp.where(place < count // 2, 2 * place, 2 * (count - 1 - place) + 1)


def gradient_kernel(
    count,
    lhs,
    hidden_t,
    rhs,
    dz_down,
    small,
    first_out,
    down_out,
    small_out,
    total,
    pair_send,
    pair_recv,
    ring_send,
    ring_recv,
    small_pair,
    small_sum,
    small_recv,
    pair_ss,
    pair_rs,
    ring_ss,
    ring_rs,
    small_sems,
    small_ss,
    small_rs,
):
    rows = first_out.shape[0]
    half_units = hidden_t.shape[0] // 2
    dp = lax.axis_index("dp")
    section = lax.axis_index("section")
    core = lax.rem(section, 2)
    peer = section + 1 - 2 * core
    place = ring_place(dp, count)

    barrier = pltpu.get_barrier_semaphore()

    def greet(step, carry):
        other = lax.rem(dp + step, count)
        pl.semaphore_signal(barrier, inc=1, device_id=(other, section), device_id_type=MESH)
        return carry

    lax.fori_loop(1, count, greet, 0)
    pl.semaphore_signal(barrier, inc=1, device_id=(dp, peer), device_id_type=MESH)
    pl.semaphore_wait(barrier, count)

    def pair_copy(step):
        return pltpu.make_async_remote_copy(
            src_ref=pair_send.at[lax.rem(step, 2)],
            dst_ref=pair_recv.at[step],
            send_sem=pair_ss.at[lax.rem(step, 2)],
            recv_sem=pair_rs.at[step],
            device_id=(dp, peer),
            device_id_type=MESH,
        )

    def ring_copy(step, stream):
        ahead = 1 if stream < 3 else count - 1
        return pltpu.make_async_remote_copy(
            src_ref=ring_send.at[lax.rem(step, 2), stream],
            dst_ref=ring_recv.at[step, stream],
            send_sem=ring_ss.at[lax.rem(step, 2), stream],
            recv_sem=ring_rs.at[step, stream],
            device_id=(ring_index(lax.rem(place + ahead, count), count), section),
            device_id_type=MESH,
        )

    def product(step, stream, part):
        if stream < 3:
            block = lax.rem(place + 2 * count - 1 - step, count)
        else:
            block = lax.rem(place + 1 + step, count)
        block = ring_index(block, count)
        if stream % 3 < 2:
            group = stream % 3 + 2 * (stream // 3)
            left_index = jnp.where(part == 1, 2, 1 if group == 3 else 0)
            left = lhs[left_index, pl.ds(pl.multiple_of(block * rows, rows), rows), :]
            right = rhs[part * 4 + group]
        else:
            start = part * half_units + block * (2 * rows) + (stream // 3) * rows
            left = hidden_t[pl.ds(pl.multiple_of(start, rows), rows), :]
            right = dz_down[...]
        return jnp.dot(left, right, preferred_element_type=jnp.float32)

    def local_part(step):
        slot = lax.rem(step, 2)

        @pl.when(step >= 2)
        def _():
            pair_copy(step - 2).wait_send()

        for stream in range(6):
            pair_send[slot, stream] = product(step, stream, 1 - core).astype(jnp.bfloat16)
        pair_copy(step).start()
        for stream in range(6):
            total[stream] = product(step, stream, core)

    gb_pair = pltpu.make_async_remote_copy(
        src_ref=small.at[1 - core],
        dst_ref=small_pair,
        send_sem=small_sems.at[0],
        recv_sem=small_sems.at[1],
        device_id=(dp, peer),
        device_id_type=MESH,
    )
    gb_pair.start()

    def gb_copy(step):
        other = lax.rem(dp + step, count)
        return pltpu.make_async_remote_copy(
            src_ref=small_sum.at[other],
            dst_ref=small_recv.at[step],
            send_sem=small_ss.at[step],
            recv_sem=small_rs.at[step],
            device_id=(other, section),
            device_id_type=MESH,
        )

    local_part(0)
    gb_pair.wait()
    small_sum[...] = small[core] + small_pair[...]

    def gb_start(step, carry):
        gb_copy(step).start()
        return carry

    lax.fori_loop(1, count, gb_start, 0)

    def ring_step(step, carry):
        slot = lax.rem(step, 2)
        pair_copy(step).wait_recv()
        for stream in (0, 3, 1, 4, 2, 5):
            total[stream] += pair_recv[step, stream].astype(jnp.float32)

            @pl.when(step >= 1)
            def _():
                ring_copy(step - 1, stream).wait_recv()
                total[stream] += ring_recv[step - 1, stream].astype(jnp.float32)

            @pl.when(step >= 2)
            def _():
                ring_copy(step - 2, stream).wait_send()

            ring_send[slot, stream] = total[stream].astype(jnp.bfloat16)
            ring_copy(step, stream).start()
        local_part(step + 1)
        return carry

    lax.fori_loop(0, count - 1, ring_step, 0)

    last = count - 1
    pair_copy(last).wait_recv()
    width = total.shape[2]
    for stream in (0, 3, 1, 4, 2, 5):
        ring_copy(last - 1, stream).wait_recv()
        value = total[stream] + pair_recv[last, stream].astype(jnp.float32)
        value = value + ring_recv[last - 1, stream].astype(jnp.float32)
        if stream % 3 < 2:
            group = stream % 3 + 2 * (stream // 3)
            first_out[:, group * width : (group + 1) * width] = value
        else:
            down_out[(stream // 3) * rows : (stream // 3 + 1) * rows, :] = value

    small_out[...] = small_sum[dp]

    def gb_finish(step, carry):
        gb_copy(step).wait()
        small_out[...] += small_recv[step]
        return carry

    lax.fori_loop(1, count, gb_finish, 0)
    for stream in range(6):
        ring_copy(last - 1, stream).wait_send()
        if count >= 3:
            ring_copy(last - 2, stream).wait_send()
    pair_copy(last).wait_send()
    pair_copy(last - 1).wait_send()


def reduce_gradients(lhs, hidden_t, rhs, dz_down, small):
    count = lax.axis_size("dp")
    width = rhs.shape[2]
    rows = width // count
    vmem = pl.BlockSpec(memory_space=pltpu.VMEM)
    sem = pltpu.SemaphoreType.DMA
    low = jnp.bfloat16
    return pl.pallas_call(
        functools.partial(gradient_kernel, count),
        out_shape=(
            jax.ShapeDtypeStruct((rows, 4 * width), jnp.float32),
            jax.ShapeDtypeStruct((2 * rows, width), jnp.float32),
            jax.ShapeDtypeStruct(small.shape[2:], jnp.float32),
        ),
        in_specs=[vmem] * 5,
        out_specs=(vmem, vmem, vmem),
        scratch_shapes=[
            pltpu.VMEM((6, rows, width), jnp.float32),
            pltpu.VMEM((2, 6, rows, width), low),
            pltpu.VMEM((count, 6, rows, width), low),
            pltpu.VMEM((2, 6, rows, width), low),
            pltpu.VMEM((count - 1, 6, rows, width), low),
            pltpu.VMEM(small.shape[1:], jnp.float32),
            pltpu.VMEM(small.shape[1:], jnp.float32),
            pltpu.VMEM(small.shape[1:], jnp.float32),
            sem((2,)),
            sem((count,)),
            sem((2, 6)),
            sem((count - 1, 6)),
            sem((2,)),
            sem((count,)),
            sem((count,)),
        ],
        compiler_params=pltpu.CompilerParams(
            collective_id=0, has_side_effects=True, vmem_limit_bytes=60 * 1024 * 1024
        ),
        name="gradients",
    )(lhs, hidden_t, rhs, dz_down, small)


def local(tokens, doc_lengths, first_weights, down_weights, norm_gains, norm_biases, cotangent):
    section_index = lax.axis_index("section")
    count = lax.axis_size("dp")
    core = section_index % 2
    late = section_index >= 2
    row_count = doc_lengths.shape[0]
    row_len = tokens.shape[0] // row_count
    width = tokens.shape[1]
    peer_first, peer_down, peer_gains, peer_biases = (
        swap_pair(first_weights[0]),
        swap_pair(down_weights[0]),
        swap_pair(norm_gains[0]),
        swap_pair(norm_biases[0]),
    )

    def ordered(own, other):
        return jnp.where(core == 0, own, other), jnp.where(core == 0, other, own)

    weight_a, weight_f = ordered(first_weights[0], peer_first)
    down_upper, down_lower = ordered(down_weights[0], peer_down)
    gains = ordered(norm_gains[0], peer_gains)
    biases = ordered(norm_biases[0], peer_biases)
    half_units = down_upper.shape[0]
    scale = HEAD ** (-0.5)
    low = jnp.bfloat16

    row = tokens.reshape(row_count, row_len, width)[core]
    row_cot = cotangent.reshape(row_count, row_len, width)[core]
    allowed = allowed_pairs(doc_lengths[core], row_len)[None]

    def scores_of(projected):
        query, key = (split_heads(projected[:, i * width : (i + 1) * width]) for i in (0, 1))
        scores = jnp.einsum("qhd,khd->hqk", query, key, preferred_element_type=jnp.float32)
        return jnp.where(allowed, scores * scale, masked_value)

    def forward(inputs):
        current = inputs.astype(jnp.float32)
        normed_a = normalize(current, gains[0][0], biases[0][0]).astype(low)
        projected = jnp.dot(
            normed_a, weight_a[:, : 3 * width], preferred_element_type=jnp.float32
        ).astype(low)
        scores = scores_of(projected)
        row_top = jnp.max(scores, axis=-1, keepdims=True)
        exponent = jnp.exp(scores - row_top)
        row_total = jnp.sum(exponent, axis=-1, keepdims=True)
        prob = (exponent / row_total).astype(low)
        context = jnp.einsum(
            "hqk,khd->qhd",
            prob,
            split_heads(projected[:, 2 * width :]),
            preferred_element_type=jnp.float32,
        )
        context = context.reshape(row_len, width).astype(low)
        branch_a = contract_cols(context, weight_a[:, 3 * width :])
        log_total = row_top + jnp.log(row_total)
        middle = (current + normalize(branch_a, gains[0][1], biases[0][1])).astype(low)
        normed_f = normalize(middle.astype(jnp.float32), gains[1][0], biases[1][0]).astype(low)
        hidden_pre = jnp.dot(normed_f, weight_f, preferred_element_type=jnp.float32)
        hidden = jax.nn.gelu(hidden_pre).astype(low)
        branch_f = jnp.dot(hidden[:, :half_units], down_upper, preferred_element_type=jnp.float32)
        branch_f = branch_f + jnp.dot(
            hidden[:, half_units:], down_lower, preferred_element_type=jnp.float32
        )
        output = middle.astype(jnp.float32) + normalize(branch_f, gains[1][1], biases[1][1])
        kept = (inputs, projected, context, log_total, branch_a, middle, hidden_pre, branch_f)
        return output.astype(low), kept

    arriving = hop(forward(row)[0], 2)
    output, kept = forward(jnp.where(late, arriving, row))
    inputs, projected, context, log_total, branch_a, middle, hidden_pre, branch_f = kept

    def backward(upstream):
        grad_out = upstream.astype(jnp.float32)
        out_back = jax.vjp(normalize, branch_f, gains[1][1], biases[1][1])[1]
        dz_f, dg_f1, db_f1 = out_back(grad_out)
        dz_f = dz_f.astype(low)
        hidden_full, gelu_back = jax.vjp(jax.nn.gelu, hidden_pre)
        d_hidden = jnp.concatenate(
            [contract_cols(dz_f, down_upper), contract_cols(dz_f, down_lower)], axis=1
        )
        d_pre = gelu_back(d_hidden)[0].astype(low)
        normed_f, in_back = jax.vjp(
            normalize, middle.astype(jnp.float32), gains[1][0], biases[1][0]
        )
        d_ln, dg_f0, db_f0 = in_back(contract_cols(d_pre, weight_f))
        d_middle = (grad_out + d_ln).astype(low)

        grad_mid = d_middle.astype(jnp.float32)
        out_back = jax.vjp(normalize, branch_a, gains[0][1], biases[0][1])[1]
        dz_a, dg_a1, db_a1 = out_back(grad_mid)
        dz_a = dz_a.astype(low)
        d_context = split_heads(
            jnp.dot(dz_a, weight_a[:, 3 * width :], preferred_element_type=jnp.float32).astype(low)
        )
        query, key, value = (
            split_heads(projected[:, i * width : (i + 1) * width]) for i in range(3)
        )
        prob = jnp.exp(scores_of(projected) - log_total)
        d_prob = jnp.einsum("qhd,khd->hqk", d_context, value, preferred_element_type=jnp.float32)
        d_value = jnp.einsum(
            "hqk,qhd->khd", prob.astype(low), d_context, preferred_element_type=jnp.float32
        )
        d_scores = prob * (d_prob - jnp.sum(d_prob * prob, axis=-1, keepdims=True))
        d_scores = d_scores.astype(low)
        d_query = scale * jnp.einsum(
            "hqk,khd->qhd", d_scores, key, preferred_element_type=jnp.float32
        )
        d_key = scale * jnp.einsum(
            "hqk,qhd->khd", d_scores, query, preferred_element_type=jnp.float32
        )
        d_proj = [v.reshape(row_len, width).astype(low) for v in (d_query, d_key, d_value)]
        normed_a, in_back = jax.vjp(
            normalize, inputs.astype(jnp.float32), gains[0][0], biases[0][0]
        )
        d_normed = contract_cols(jnp.concatenate(d_proj, axis=1), weight_a[:, : 3 * width])
        d_ln, dg_a0, db_a0 = in_back(d_normed)
        d_input = (grad_mid + d_ln).astype(low)
        small = jnp.stack([dg_a0, dg_a1, db_a0, db_a1, dg_f0, dg_f1, db_f0, db_f1])
        lhs = jnp.stack([normed_a.astype(low).T, dz_a.T, normed_f.astype(low).T])
        rhs = jnp.stack(d_proj + [context] + jnp.split(d_pre, 4, axis=1))
        return d_input, (lhs, hidden_full.astype(low).T, rhs, dz_f, small, d_middle)

    arriving = hop(backward(row_cot)[0], -2)
    d_input, parts = backward(jnp.where(late, row_cot, arriving))
    lhs, hidden_t, rhs, dz_f, small, d_middle = parts

    slices = small.reshape(2, 4, count, width // count).transpose(0, 2, 1, 3)
    slices = jnp.pad(slices, ((0, 0), (0, 0), (0, 4), (0, 128 - width // count)))
    first_part, down_part, small_part = reduce_gradients(lhs, hidden_t, rhs, dz_f, slices)
    small_part = small_part[:4, : width // count].reshape(2, 2, width // count)

    def both_rows(for_attention, for_feed):
        own = jnp.where(core == 0, for_attention, for_feed)
        other = swap_pair(jnp.where(core == 0, for_feed, for_attention))
        return jnp.concatenate(ordered(own, other), axis=0)

    return (
        both_rows(middle, output)[None],
        both_rows(d_input, d_middle)[None],
        first_part[None],
        down_part[None],
        small_part[0][None],
        small_part[1][None],
    )


def solution(mesh):
    placed = (
        P("dp", None),
        P("dp", None),
        P("section", None, None),
        P("section", None, None),
        P("section", None, None),
        P("section", None, None),
        P("dp", None),
    )
    return jax.shard_map(
        local,
        mesh=mesh,
        in_specs=placed,
        out_specs=(
            P("section", "dp", None),
            P("section", "dp", None),
            P("section", "dp", None),
            P("section", "dp", None),
            P("section", None, "dp"),
            P("section", None, "dp"),
        ),
        check_vma=False,
    )
```

time: 1700 us -> 579 us (0.34)
  waiting for transfers between devices: 943 us -> 54.2 us
  starting transfers between devices: 197 us -> 7.24 us
  Pallas kernels: 0 us -> 137 us
  local copies, waits for them, and re-layouts: 160 us -> 61.3 us
  other arithmetic: 189 us -> 112 us
  matrix products: 150 us -> 196 us
  loops' own time: 26.4 us -> 0 us
    reduce_scatter x2 -> x0, waiting for transfers between devices: 437 us -> none  [the longest x1 286 us: local(): lax.psum_scatter(acc_first, 'dp', scatter_dimension=0, tiled=True)]
    ppermute x12 -> x8, waiting for transfers between devices: 413 us -> 54.2 us  [the longest x2 39.3 us: hop(): return lax.ppermute(value, 'section', pairs)]
    ppermute x12 -> x8, starting transfers between devices: 196 us -> 7.24 us  [the longest x2 6.12 us: hop(): return lax.ppermute(value, 'section', pairs)]
    pallas_call x0 -> x1, Pallas kernels: none -> 137 us  [reduce_gradients(): pl.pallas_call(functools.partial(gradient_kernel, count), out_shape=(jax....]
    unnamed x6 -> x0, waiting for transfers between devices: 93.4 us -> none
    scatter x10 -> x0, other arithmetic: 50.1 us -> none  [the longest x2 25.2 us: forward_run_rows(): kept_big.at[slot_index].set(big_rows)]
    dot_general x4 -> x10, matrix products: 22 us -> 54.5 us  [contract_cols(): lax.dot_general(left, right, (((1,), (1,)), ((), ())), preferred_element_...]
    cond x110 -> x0, local copies, waits for them, and re-layouts: 30.2 us -> none
  transfers between devices with their start and end apart: 16 -> 8, of which waited for: 16 -> 4; matrix products, arithmetic and copies ran while one was open for 2% -> 24% of each run, Pallas kernels for 0% -> 24%
where the time goes in v1:
time: 579 us; the launch traced here: 569 us
  matrix products  196 us (34%)
  Pallas kernels  137 us (24%)
  other arithmetic  112 us (19%)
  local copies, waits for them, and re-layouts  61.3 us (11%)
  waiting for transfers between devices  54.2 us (9%)
  starting transfers between devices  7.24 us (1%)
    pallas_call x1, Pallas kernels, reduce_gradients(): pl.pallas_call(functools.partial(gradient_kernel, count), out_shape=(jax....  137 us
    dot_general x10, matrix products, contract_cols(): lax.dot_general(left, right, (((1,), (1,)), ((), ())), preferred_element_...  54.5 us
    ppermute x2, waiting for transfers between devices, hop(): return lax.ppermute(value, 'section', pairs)  39.3 us
    convert_element_type x2, other arithmetic, backward(): d_scores = d_scores.astype(low)  25.3 us
    dot_general x2, matrix products, backward(): jnp.einsum('qhd,khd->hqk', d_context, value, preferred_element_type=jnp.f...  24.5 us
    dot_general x2, matrix products, forward(): hidden_pre = jnp.dot(normed_f, weight_f, preferred_element_type=jnp.float32)  22.7 us
    dot_general x2, matrix products, backward(): jnp.einsum('hqk,qhd->khd', prob.astype(low), d_context, preferred_element...  20.5 us
    unnamed x138, local copies, waits for them, and re-layouts  19.2 us
  transfers between devices with their start and end apart: 8, of which 4 were waited for; matrix products, arithmetic and copies ran while one was open for 24% of the time, Pallas kernels for 24%

profile of v1, /device:TPU:0, one launch (start us, length us, event | category | flops | bytes accessed | tf_op | source)
XLA Modules:
  0.0 569.4 jit_solution(8589319800940836722)
XLA Ops:
  7.6 12.7 %collective-permute-done.3 = bf16[2048,1024]{1,0:T(8,128)(2,1)} collective-permute-done((bf16[2048,1024]{1,0:T(8,128)(2,1)}, bf16[2048,1024]{1,0:T(8,128)(2,1)}, u32[]{:S(2)}, u32[]{:S(2)}) %collective-permute-start.3) | collective-permute-done | bytes 4194336 | tf_op jit(solution)/shard_map/ppermute | solution.py:19
  20.3 5.7 %broadcast_select_fusion.3 = (bf16[2048,1024]{1,0:T(8,128)(2,1)}, bf16[2048,1024]{1,0:T(8,128)(2,1)}) fusion(bf16[2048,1024]{1,0:T(8,128)(2,1)} %collective-permute-done.3, pred[]{:T(512)S(6)} %eq.14, bf16[1,2048,1024]{2,1,0:T(8,128)(2,1)} %param.10), kind=kLoop, calls=%fused_computation.60 | loop fusion | flops 4194304 | bytes 16777216 | tf_op jit(solution)/shard_map/jit(_where)/select_n | solution.py:294
  26.1 9.2 %broadcast_select_fusion = (bf16[1024,4096]{1,0:T(8,128)(2,1)}, bf16[1024,4096]{1,0:T(8,128)(2,1)S(1)}) fusion(bf16[1024,4096]{1,0:T(8,128)(2,1)} %collective-permute-done.2, pred[]{:T(512)S(6)} %eq.14, bf16[1,1024,4096]{2,1,0:T(8,128)(2,1)} %param.9), kind=kLoop, calls=%fused_computation.48 | loop fusion | flops 8388608 | bytes 33554432 | tf_op jit(solution)/shard_map/jit(_where)/select_n | solution.py:294
  35.2 4.0 convolution_convert_fusion.1
  46.7 10.8 %fusion.211 = (f32[16,512]{1,0:T(8,128)S(1)}, f32[16,512,512]{1,2,0:T(8,128)}) fusion(pred[512,512]{0,1:T(8,128)(4,1)S(1)} %fusion.161, bf16[512,16,64]{0,2,1:T(8,128)(2,1)} %bitcast.219, bf16[512,16,64]{0,2,1:T(8,128)(2,1)} %bitcast.220), kind=kOutput, calls=%fused_computation.334 | convolution fusion | flops 553648640 | bytes 19169280 | tf_op jit(solution)/shard_map/sub | solution.py:321
  57.5 7.4 %fusion.129 = bf16[16,64,512]{2,1,0:T(8,128)(2,1)S(1)} fusion(bf16[512,16,64]{0,2,1:T(8,128)(2,1)S(1)} %bitcast.221, f32[16,512,512]{1,2,0:T(8,128)} %get-tuple-element.80, f32[16,512]{1,0:T(8,128)S(1)} %get-tuple-element.79), kind=kOutput, calls=%fused_computation.199 | convolution fusion | flops 545783808 | bytes 18907136 | tf_op jit(solution)/shard_map/hqk,khd->qhd/dot_general | solution.py:324
  65.0 3.0 fusion.212
  69.5 10.4 %fusion.15 = bf16[512,4096]{1,0:T(8,128)(2,1)S(1)} fusion(bf16[1024,4096]{1,0:T(8,128)(2,1)} %get-tuple-element.46, bf16[512,1024]{1,0:T(8,128)(2,1)S(1)} %get-tuple-element.45, f32[1024]{0:T(1024)S(1)} %bitcast.264, f32[1024]{0:T(1024)S(1)} %bitcast.239, f32[512]{0:T(512)S(1)} %add_rsqrt_fusion.1, f32[512]{0:T(512)S(1)} %broadcast_multiply_fusion.5), kind=kOutput, calls=%fused_computation.30 | convolution fusion | flops 4316987392 | bytes 13643776 | tf_op jit(solution)/shard_map/dot_general | solution.py:335
  82.4 2.4 fusion.213
  85.8 4.8 collective-permute-start.4
  90.6 22.6 %collective-permute-done.4 = bf16[512,1024]{1,0:T(8,128)(2,1)S(1)} collective-permute-done((bf16[512,1024]{1,0:T(8,128)(2,1)S(1)}, bf16[512,1024]{1,0:T(8,128)(2,1)S(1)}, u32[]{:S(2)}, u32[]{:S(2)}) %collective-permute-start.4) | collective-permute-done | bytes 1048608 | tf_op jit(solution)/shard_map/ppermute | solution.py:25
  115.3 7.0 %convolution_convert_fusion = bf16[512,3072]{1,0:T(8,128)(2,1)S(1)} fusion(bf16[1024,4096]{1,0:T(8,128)(2,1)} %copy-done.21, bf16[512,1024]{1,0:T(8,128)(2,1)S(1)} %get-tuple-element.43, f32[512]{0:T(512)S(1)} %fusion.163, f32[512]{0:T(512)S(1)} %broadcast_multiply_fusion.3, f32[1024]{0:T(1024)S(1)} %bitcast.268, f32[1024]{0:T(1024)S(1)} %bitcast.248), kind=kOutput, calls=%fused_computation.53 | convolution fusion | flops 3225944064 | bytes 10498048 | tf_op jit(solution)/shard_map/dot_general | solution.py:316
  126.3 7.4 %fusion.3 = (f32[16,512]{1,0:T(8,128)S(1)}, f32[16,512,512]{1,2,0:T(8,128)}) fusion(pred[512,512]{0,1:T(8,128)(4,1)S(1)} %fusion.161, bf16[512,16,64]{0,2,1:T(8,128)(2,1)S(1)} %bitcast.182, bf16[512,16,64]{0,2,1:T(8,128)(2,1)S(1)} %bitcast.179), kind=kOutput, calls=%fused_computation.18 | convolution fusion | flops 549445632 | bytes 19169280 | tf_op jit(solution)/shard_map/qhd,khd->hqk/dot_general | solution.py:310
  133.8 9.5 %fusion.1 = f32[16,512]{1,0:T(8,128)S(1)} fusion(f32[16,512,512]{1,2,0:T(8,128)} %get-tuple-element.86, f32[16,512]{1,0:T(8,128)S(1)} %get-tuple-element.85, pred[512,512]{0,1:T(8,128)(4,1)S(1)} %fusion.161), kind=kLoop, calls=%fused_computation.12 | loop fusion | flops 16769024 | bytes 17104896 | tf_op jit(solution)/shard_map/reduce_sum | solution.py:322
  143.9 9.3 %fusion.128 = bf16[16,64,512]{2,1,0:T(8,128)(2,1)S(1)} fusion(bf16[512,16,64]{0,2,1:T(8,128)(2,1)S(1)} %bitcast.185, f32[16,512,512]{1,2,0:T(8,128)} %get-tuple-element.86, f32[16,512]{1,0:T(8,128)S(1)} %fusion.1, f32[16,512]{1,0:T(8,128)S(1)} %get-tuple-element.85, pred[512,512]{0,1:T(8,128)(4,1)S(1)} %fusion.161), kind=kOutput, calls=%fused_computation.198 | convolution fusion | flops 558366720 | bytes 19202048 | tf_op jit(solution)/shard_map/hqk,khd->qhd/dot_general | solution.py:324
  153.1 3.4 fusion.214
  158.3 12.3 %multiply_convert_fusion.2 = (bf16[512,4096]{1,0:T(8,128)(2,1)S(1)}, f32[512,4096]{1,0:T(8,128)}) fusion(bf16[1024,4096]{1,0:T(8,128)(2,1)} %get-tuple-element.46, bf16[512,1024]{1,0:T(8,128)(2,1)S(1)} %get-tuple-element.41, f32[512]{0:T(512)S(1)} %fusion.165, f32[512]{0:T(512)S(1)} %broadcast_multiply_fusion.1, f32[1024]{0:T(1024)S(1)} %bitcast.265, ...), kind=kOutput, calls=%fused_computation.44 | convolution fusion | flops 4316987392 | bytes 22032384 | tf_op jit(solution)/shard_map/dot_general | solution.py:335
  176.9 4.3 fusion.183
  181.2 4.3 fusion.182
  185.5 15.7 %fusion.105 = (f32[512]{0:T(512)S(1)}, f32[512,1024]{1,0:T(8,128)}) fusion(bf16[512,1024]{1,0:T(8,128)(2,1)S(1)} %get-tuple-element.41, f32[512]{0:T(512)S(1)} %broadcast_multiply_fusion.1, f32[1024]{0:T(1024)S(1)} %bitcast.241, bf16[1024,4096]{1,0:T(8,128)(2,1)} %get-tuple-element.46, f32[512,4096]{1,0:T(8,128)} %get-tuple-element.90, ...), kind=kOutput, calls=%fused_computation.166 | convolution fusion | flops 4341628416 | bytes 28319744 | tf_op jit(solution)/shard_map/dot_general | solution.py:47
  201.3 2.5 fusion.191
  203.8 2.9 fusion.94
  207.8 4.1 convolution_convert_fusion.3
  214.1 12.3 %multiply_reduce_fusion.1 = (f32[16,512]{1,0:T(8,128)S(1)}, f32[16,512,512]{1,2,0:T(8,128)}) fusion(f32[16,512]{1,0:T(8,128)S(1)} %log_add_fusion, f32[16,512,512]{1,2,0:T(8,128)} %get-tuple-element.86, pred[512,512]{0,1:T(8,128)(4,1)S(1)} %fusion.161, bf16[512,16,64]{0,2,1:T(8,128)(2,1)} %bitcast.209, bf16[512,16,64]{0,2,1:T(8,128)(2,1)} %bitcast.186), kind=kOutput, calls=%fused_computation.4 | convolution fusion | flops 557834240 | bytes 35979264 | tf_op jit(solution)/shard_map/qhd,khd->hqk/dot_general | solution.py:376
  226.4 12.6 %multiply_convert_fusion.1 = bf16[16,512,512]{1,2,0:T(8,128)(2,1)S(1)} fusion(f32[16,512,512]{1,2,0:T(8,128)} %get-tuple-element.96, f32[16,512]{1,0:T(8,128)S(1)} %get-tuple-element.95, f32[16,512]{1,0:T(8,128)S(1)} %log_add_fusion, f32[16,512,512]{1,2,0:T(8,128)} %get-tuple-element.86, pred[512,512]{0,1:T(8,128)(4,1)S(1)} %fusion.161), kind=kLoop, calls=%fused_computation.3 | loop fusion | flops 25165824 | bytes 42270720 | tf_op jit(solution)/shard_map/convert_element_type | solution.py:381
  239.1 2.5 multiply_convert_fusion.6
  241.6 3.6 multiply_convert_fusion.5
  245.2 8.9 %fusion.130 = bf16[16,64,512]{2,1,0:T(8,128)(2,1)} fusion(bf16[512,16,64]{0,2,1:T(8,128)(2,1)S(1)} %bitcast.210, f32[16,512,512]{1,2,0:T(8,128)} %get-tuple-element.86, f32[16,512]{1,0:T(8,128)S(1)} %log_add_fusion, pred[512,512]{0,1:T(8,128)(4,1)S(1)} %fusion.161), kind=kOutput, calls=%fused_computation.202 | convolution fusion | flops 554172416 | bytes 19169280 | tf_op jit(solution)/shard_map/hqk,qhd->khd/dot_general | solution.py:377
  254.1 9.0 %copy.82 = f32[512,4096]{0,1:T(8,128)} copy(f32[512,4096]{1,0:T(8,128)} %get-tuple-element.90) | data formatting | bytes 16777216 | tf_op jit(solution)/shard_map/dot_general | solution.py:335
  265.7 6.5 %fusion.101 = (f32[512]{0:T(512)S(1)}, f32[512,1024]{1,0:T(8,128)S(1)}) fusion(bf16[512,1024]{1,0:T(8,128)(2,1)S(1)} %copy-done.6, f32[512]{0:T(512)S(1)} %broadcast_multiply_fusion.3, f32[1024]{0:T(1024)S(1)} %bitcast.249, bf16[1024,4096]{1,0:T(8,128)(2,1)} %copy-done.21, bf16[512,1024]{0,1:T(8,128)(2,1)S(1)} %bitcast.277, ...), kind=kOutput, calls=%fused_computation.162 | convolution fusion | flops 3233283584 | bytes 12591104 | tf_op jit(solution)/shard_map/dot_general | solution.py:47
  277.2 2.5 copy.86
  279.7 6.2 %fusion.23.hidden_t = bf16[4096,512]{1,0:T(8,128)(2,1)} fusion(f32[512,4096]{0,1:T(8,128)} %copy.82), kind=kLoop, calls=%fused_computation.38 | loop fusion | flops 18874368 | bytes 12582912 | tf_op jit(solution)/shard_map/convert_element_type | solution.py:336
  285.9 16.7 %collective-permute-done.6 = bf16[512,1024]{1,0:T(8,128)(2,1)} collective-permute-done((bf16[512,1024]{1,0:T(8,128)(2,1)}, bf16[512,1024]{1,0:T(8,128)(2,1)}, u32[]{:S(2)}, u32[]{:S(2)}) %collective-permute-start.6) | collective-permute-done | bytes 1048608 | tf_op jit(solution)/shard_map/ppermute | solution.py:25
  307.1 4.3 fusion.216
  311.4 4.3 fusion.217
  315.7 8.3 %add_convert_fusion = bf16[512,4096]{1,0:T(8,128)(2,1)S(1)} fusion(f32[512,4096]{1,0:T(8,128)S(1)} %bitcast.178, f32[512,2048]{1,0:T(8,128)} %fusion.217, f32[512,2048]{1,0:T(8,128)} %fusion.216), kind=kLoop, calls=%fused_computation.41 | loop fusion | flops 44040192 | bytes 20971520 | tf_op jit(solution)/shard_map/convert_element_type | solution.py:358
  324.1 4.8 fusion.195
  330.5 2.8 fusion.111
  335.6 3.9 convolution_convert_fusion.2
  341.7 12.3 %multiply_reduce_fusion = (f32[16,512]{1,0:T(8,128)S(1)}, f32[16,512,512]{1,2,0:T(8,128)}) fusion(f32[16,512]{1,0:T(8,128)S(1)} %log_add_fusion, f32[16,512,512]{1,2,0:T(8,128)} %get-tuple-element.86, pred[512,512]{0,1:T(8,128)(4,1)S(1)} %fusion.161, bf16[512,16,64]{0,2,1:T(8,128)(2,1)} %bitcast.207, bf16[512,16,64]{0,2,1:T(8,128)(2,1)} %bitcast.187), kind=kOutput, calls=%fused_computation.2 | convolution fusion | flops 557834240 | bytes 35979264 | tf_op jit(solution)/shard_map/qhd,khd->hqk/dot_general | solution.py:376
  354.0 12.7 %multiply_convert_fusion = bf16[16,512,512]{1,2,0:T(8,128)(2,1)S(1)} fusion(f32[16,512,512]{1,2,0:T(8,128)} %get-tuple-element.101, f32[16,512]{1,0:T(8,128)S(1)} %get-tuple-element.100, f32[16,512]{1,0:T(8,128)S(1)} %log_add_fusion, f32[16,512,512]{1,2,0:T(8,128)} %get-tuple-element.86, pred[512,512]{0,1:T(8,128)(4,1)S(1)} %fusion.161), kind=kLoop, calls=%fused_computation.1 | loop fusion | flops 25165824 | bytes 42270720 | tf_op jit(solution)/shard_map/convert_element_type | solution.py:381
  368.2 2.6 multiply_convert_fusion.3
  370.8 11.6 %fusion.133 = bf16[16,64,512]{2,1,0:T(8,128)(2,1)} fusion(bf16[512,16,64]{0,2,1:T(8,128)(2,1)} %bitcast.208, f32[16,512,512]{1,2,0:T(8,128)} %get-tuple-element.86, f32[16,512]{1,0:T(8,128)S(1)} %log_add_fusion, pred[512,512]{0,1:T(8,128)(4,1)S(1)} %fusion.161), kind=kOutput, calls=%fused_computation.203 | convolution fusion | flops 554172416 | bytes 19169280 | tf_op jit(solution)/shard_map/hqk,qhd->khd/dot_general | solution.py:377
  384.3 3.8 fusion.196
  398.8 3.8 pad_maximum_fusion.2
  402.7 4.7 copy.88.lhs
  407.3 5.4 broadcast_select_fusion.6
  421.0 136.9 %gradients.1 = (f32[128,4096]{1,0:T(8,128)}, f32[256,1024]{1,0:T(8,128)}, f32[8,128]{1,0:T(8,128)}) custom-call(bf16[3,1024,512]{2,1,0:T(8,128)(2,1)} %copy.88.lhs, bf16[4096,512]{1,0:T(8,128)(2,1)} %fusion.23.hidden_t, bf16[8,512,1024]{2,1,0:T(8,128)(2,1)} %fusion.147.rhs, bf16[512,1024]{1,0:T(8,128)(2,1)} %copy-done.38, f32[2,8,8,128]{3,2,1,0:T(8,128)} %pad.4.small), custom_call_target="tpu_custom_call" | custom-call | tf_op jit(solution)/shard_map/gradients/pallas_call | solution.py:245
  (245 shorter events, 88.8 us)
Async XLA Ops:
  0.6 6.9 %copy-start.55 = (f32[1,2,1024]{2,1,0:T(2,128)S(1)}, f32[1,2,1024]{2,1,0:T(2,128)}, u32[]{:S(2)}) copy-start(f32[1,2,1024]{2,1,0:T(2,128)} %param.11) | copy-start | bytes 24580
  0.7 6.9 %copy-start.54 = (f32[1,2,1024]{2,1,0:T(2,128)S(1)}, f32[1,2,1024]{2,1,0:T(2,128)}, u32[]{:S(2)}) copy-start(f32[1,2,1024]{2,1,0:T(2,128)} %param.12) | copy-start | bytes 24580
  0.7 25.4 %collective-permute-start.2 = (bf16[1024,4096]{1,0:T(8,128)(2,1)}, bf16[1024,4096]{1,0:T(8,128)(2,1)}, u32[]{:S(2)}, u32[]{:S(2)}) collective-permute-start(bf16[1024,4096]{1,0:T(8,128)(2,1)} %bitcast.188), channel_id=1, source_target_pairs={{0,1},{1,0},{2,3},{3,2},{4,5},{5,4},{6,7},{7,6},{8,9},{9,8},{10,11... | collective-permute-start | bytes 25165832 | tf_op jit(solution)/shard_map/ppermute | solution.py:19
  1.2 19.1 %collective-permute-start.3 = (bf16[2048,1024]{1,0:T(8,128)(2,1)}, bf16[2048,1024]{1,0:T(8,128)(2,1)}, u32[]{:S(2)}, u32[]{:S(2)}) collective-permute-start(bf16[2048,1024]{1,0:T(8,128)(2,1)} %bitcast.204), channel_id=1, source_target_pairs={{0,1},{1,0},{2,3},{3,2},{4,5},{5,4},{6,7},{7,6},{8,9},{9,8},{10,11... | collective-permute-start | bytes 12582920 | tf_op jit(solution)/shard_map/ppermute | solution.py:19
  1.3 6.2 %collective-permute-start = (f32[2,1024]{1,0:T(2,128)}, f32[2,1024]{1,0:T(2,128)S(1)}, u32[]{:S(2)}, u32[]{:S(2)}) collective-permute-start(f32[2,1024]{1,0:T(2,128)} %bitcast.273), channel_id=1, source_target_pairs={{0,1},{1,0},{2,3},{3,2},{4,5},{5,4},{6,7},{7,6},{8,9},{9,8},{10,11... | collective-permute-start | bytes 24584 | tf_op jit(solution)/shard_map/ppermute | solution.py:19
  1.7 5.8 %collective-permute-start.1 = (f32[2,1024]{1,0:T(2,128)}, f32[2,1024]{1,0:T(2,128)S(1)}, u32[]{:S(2)}, u32[]{:S(2)}) collective-permute-start(f32[2,1024]{1,0:T(2,128)} %bitcast.272), channel_id=1, source_target_pairs={{0,1},{1,0},{2,3},{3,2},{4,5},{5,4},{6,7},{7,6},{8,9},{9,8},{10,11... | collective-permute-start | bytes 24584 | tf_op jit(solution)/shard_map/ppermute | solution.py:19
  7.6 77.6 %copy-start.50 = (f32[1,1024]{1,0:T(1,128)}, f32[1,1024]{1,0:T(1,128)S(1)}, u32[]{:S(2)}) copy-start(f32[1,1024]{1,0:T(1,128)S(1)} %get-tuple-element.69) | copy-start | bytes 12292
  26.1 9.2 %copy-start.22 = (bf16[1024,1024]{1,0:T(8,128)(2,1)S(1)}, bf16[1024,1024]{1,0:T(8,128)(2,1)}, u32[]{:S(2)}) copy-start(bf16[1024,1024]{1,0:T(8,128)(2,1)} %param.7) | copy-start | bytes 6291460
  35.2 4.0 copy-start.21
  46.7 10.8 %copy-start.49 = (bf16[512,1024]{0,1:T(8,128)(2,1)S(1)}, bf16[512,1024]{0,1:T(8,128)(2,1)}, u32[]{:S(2)}) copy-start(bf16[512,1024]{0,1:T(8,128)(2,1)} %copy.66) | copy-start | bytes 3145732
  69.5 10.5 %copy-start.29 = (bf16[2048,1024]{1,0:T(8,128)(2,1)S(1)}, bf16[2048,1024]{1,0:T(8,128)(2,1)}, u32[]{:S(2)}) copy-start(bf16[2048,1024]{1,0:T(8,128)(2,1)} %get-tuple-element.49) | copy-start | bytes 12582916
  85.8 27.5 %collective-permute-start.4 = (bf16[512,1024]{1,0:T(8,128)(2,1)S(1)}, bf16[512,1024]{1,0:T(8,128)(2,1)S(1)}, u32[]{:S(2)}, u32[]{:S(2)}) collective-permute-start(bf16[512,1024]{1,0:T(8,128)(2,1)S(1)} %fusion.99), channel_id=1, source_target_pairs={{0,2},{1,3},{4,6},{5,7},{8,10},{9,11},{12,14},{13,15},{16,18},{17,... | collective-permute-start | bytes 3145736 | tf_op jit(solution)/shard_map/ppermute | solution.py:25
  114.8 42.0 %copy-start.5 = (bf16[512,1024]{1,0:T(8,128)(2,1)}, bf16[512,1024]{1,0:T(8,128)(2,1)S(1)}, u32[]{:S(2)}) copy-start(bf16[512,1024]{1,0:T(8,128)(2,1)S(1)} %get-tuple-element.43) | copy-start | bytes 3145732
  115.3 7.0 %copy-start.52 = (f32[512]{0:T(512)}, f32[512]{0:T(512)S(1)}, u32[]{:S(2)}) copy-start(f32[512]{0:T(512)S(1)} %fusion.100) | copy-start | bytes 6148
  124.4 9.3 %copy-start.13 = (bf16[512,1024]{0,1:T(8,128)(2,1)}, bf16[512,1024]{0,1:T(8,128)(2,1)S(1)}, u32[]{:S(2)}) copy-start(bf16[512,1024]{0,1:T(8,128)(2,1)S(1)} %copy.71) | copy-start | bytes 3145732
  126.3 7.4 %copy-start.8 = (bf16[512,1024]{0,1:T(8,128)(2,1)}, bf16[512,1024]{0,1:T(8,128)(2,1)S(1)}, u32[]{:S(2)}) copy-start(bf16[512,1024]{0,1:T(8,128)(2,1)S(1)} %copy.72) | copy-start | bytes 3145732
  133.8 9.5 %copy-start.41 = (bf16[512,1024]{1,0:T(8,128)(2,1)S(1)}, bf16[512,1024]{1,0:T(8,128)(2,1)}, u32[]{:S(2)}) copy-start(bf16[512,1024]{1,0:T(8,128)(2,1)} %get-tuple-element.56) | copy-start | bytes 3145732
  143.9 9.3 %copy-start.18 = (bf16[512,1024]{0,1:T(8,128)(2,1)}, bf16[512,1024]{0,1:T(8,128)(2,1)S(1)}, u32[]{:S(2)}) copy-start(bf16[512,1024]{0,1:T(8,128)(2,1)S(1)} %copy.70) | copy-start | bytes 3145732
  153.1 3.4 copy-start.46
  158.3 12.3 %copy-start.30 = (bf16[2048,1024]{1,0:T(8,128)(2,1)S(1)}, bf16[2048,1024]{1,0:T(8,128)(2,1)}, u32[]{:S(2)}) copy-start(bf16[2048,1024]{1,0:T(8,128)(2,1)} %get-tuple-element.49) | copy-start | bytes 12582916
  201.3 2.5 copy-start.3
  226.4 12.6 %copy-start.9 = (bf16[512,1024]{0,1:T(8,128)(2,1)S(1)}, bf16[512,1024]{0,1:T(8,128)(2,1)}, u32[]{:S(2)}) copy-start(bf16[512,1024]{0,1:T(8,128)(2,1)} %copy-done.8) | copy-start | bytes 3145732
  239.1 2.5 copy-start.14
  241.6 3.6 copy-start.36
  254.1 9.0 %copy-start.51 = (f32[1,1024]{1,0:T(1,128)S(1)}, f32[1,1024]{1,0:T(1,128)}, u32[]{:S(2)}) copy-start(f32[1,1024]{1,0:T(1,128)} %copy-done.50) | copy-start | bytes 12292
  263.2 2.5 copy-start.57
  265.7 6.5 %copy-start.53 = (f32[512]{0:T(512)S(1)}, f32[512]{0:T(512)}, u32[]{:S(2)}) copy-start(f32[512]{0:T(512)} %copy-done.52) | copy-start | bytes 6148
  275.9 26.7 %collective-permute-start.6 = (bf16[512,1024]{1,0:T(8,128)(2,1)}, bf16[512,1024]{1,0:T(8,128)(2,1)}, u32[]{:S(2)}, u32[]{:S(2)}) collective-permute-start(bf16[512,1024]{1,0:T(8,128)(2,1)} %get-tuple-element.61), channel_id=1, source_target_pairs={{2,0},{3,1},{6,4},{7,5},{10,8},{11,9},{14,12},{15,13},{18,16},{19,... | collective-permute-start | bytes 3145736 | tf_op jit(solution)/shard_map/ppermute | solution.py:25
  279.7 22.9 %copy-start.24 = (bf16[1024,1024]{1,0:T(8,128)(2,1)S(1)}, bf16[1024,1024]{1,0:T(8,128)(2,1)}, u32[]{:S(2)}) copy-start(bf16[1024,1024]{1,0:T(8,128)(2,1)} %param.13) | copy-start | bytes 6291460
  279.7 278.2 %collective-permute-start.5 = (bf16[512,1024]{1,0:T(8,128)(2,1)}, bf16[512,1024]{1,0:T(8,128)(2,1)}, u32[]{:S(2)}, u32[]{:S(2)}) collective-permute-start(bf16[512,1024]{1,0:T(8,128)(2,1)} %broadcast_select_fusion.10), channel_id=1, source_target_pairs={{0,1},{1,0},{2,3},{3,2},{4,5},{5,4},{6,7},{7,6},{8,9},{9,8},{10,11... | collective-permute-start | bytes 3145736 | tf_op jit(solution)/shard_map/ppermute | solution.py:19
  307.1 4.3 copy-start.38
  307.1 4.3 copy-start.31
  307.1 8.7 %slice-start = ((s8[8388608]{0:T(1024)(128)(4,1)}), s8[4194304]{0:T(1024)(128)(4,1)S(1)}, s32[]{:S(2)}) async-start(s8[8388608]{0:T(1024)(128)(4,1)} %bitcast.177), calls=%async_computation | async-start | bytes 8388608
  311.4 4.4 slice-start.1
  311.4 12.7 %slice-start.4 = ((s8[8388608]{0:T(1024)(128)(4,1)}), s8[4194304]{0:T(1024)(128)(4,1)S(1)}, s32[]{:S(2)}) async-start(s8[8388608]{0:T(1024)(128)(4,1)} %bitcast.191), calls=%async_computation.4 | async-start | bytes 8388608
  315.7 8.3 %slice-start.5 = ((s8[8388608]{0:T(1024)(128)(4,1)}), s8[4194304]{0:T(1024)(128)(4,1)S(1)}, s32[]{:S(2)}) async-start(s8[8388608]{0:T(1024)(128)(4,1)} %bitcast.191), calls=%async_computation.5 | async-start | bytes 8388608
  324.1 4.8 copy-start.11
  354.0 12.7 %copy-start.10 = (bf16[512,1024]{0,1:T(8,128)(2,1)S(1)}, bf16[512,1024]{0,1:T(8,128)(2,1)}, u32[]{:S(2)}) copy-start(bf16[512,1024]{0,1:T(8,128)(2,1)} %copy-done.8) | copy-start | bytes 3145732
  368.2 15.4 %copy-start.28 = (bf16[16,64,512]{2,1,0:T(8,128)(2,1)}, bf16[16,64,512]{2,1,0:T(8,128)(2,1)S(1)}, u32[]{:S(2)}) copy-start(bf16[16,64,512]{2,1,0:T(8,128)(2,1)S(1)} %multiply_convert_fusion.4) | copy-start | bytes 3145732
  368.2 15.4 %slice-start.2 = ((s8[8388608]{0:T(1024)(128)(4,1)}), s8[4194304]{0:T(1024)(128)(4,1)S(1)}, s32[]{:S(2)}) async-start(s8[8388608]{0:T(1024)(128)(4,1)} %bitcast.189), calls=%async_computation.2 | async-start | bytes 8388608
  370.8 12.8 %copy-start.35 = (bf16[16,64,512]{2,1,0:T(8,128)(2,1)}, bf16[16,64,512]{2,1,0:T(8,128)(2,1)S(1)}, u32[]{:S(2)}) copy-start(bf16[16,64,512]{2,1,0:T(8,128)(2,1)S(1)} %multiply_convert_fusion.3) | copy-start | bytes 3145732
  370.8 11.6 %copy-start.27 = (f32[512,1024]{1,0:T(8,128)S(1)}, f32[512,1024]{1,0:T(8,128)}, u32[]{:S(2)}) copy-start(f32[512,1024]{1,0:T(8,128)} %copy-done.26) | copy-start | bytes 6291460
  370.8 12.8 %slice-start.3 = ((s8[8388608]{0:T(1024)(128)(4,1)}), s8[4194304]{0:T(1024)(128)(4,1)S(1)}, s32[]{:S(2)}) async-start(s8[8388608]{0:T(1024)(128)(4,1)} %bitcast.189), calls=%async_computation.3 | async-start | bytes 8388608
  407.3 6.1 %copy-start.39 = (bf16[1,512,1024]{2,1,0:T(8,128)(2,1)S(1)}, bf16[1,512,1024]{2,1,0:T(8,128)(2,1)}, u32[]{:S(2)}) copy-start(bf16[1,512,1024]{2,1,0:T(8,128)(2,1)} %copy.84) | copy-start | bytes 3145732
  412.7 149.5 %collective-permute-start.7 = (bf16[512,1024]{1,0:T(8,128)(2,1)}, bf16[512,1024]{1,0:T(8,128)(2,1)}, u32[]{:S(2)}, u32[]{:S(2)}) collective-permute-start(bf16[512,1024]{1,0:T(8,128)(2,1)} %get-tuple-element.28), channel_id=1, source_target_pairs={{0,1},{1,0},{2,3},{3,2},{4,5},{5,4},{6,7},{7,6},{8,9},{9,8},{10,11... | collective-permute-start | bytes 3145736 | tf_op jit(solution)/shard_map/ppermute | solution.py:19
  412.7 2.8 copy-start.37
  413.4 3.2 copy-start.12
  566.3 2.9 copy-start.1
  (24 other events, 41.8 us)
